TPU v7x, 32 devices: a whole 2x2x4 slice. The times are simulated.
32 devices in a mesh: branch: 4 (over z), dp: 8 (over y, x, core).
Axes of the slice: x: 2, y: 2, z: 4, core: 2. Of those that a mesh axis runs over, the one named last changes fastest.
Arguments:
- tokens: bfloat16 [64, 4096], P('dp'), may hold values from -6 to 6
- routes: int32 [64, 2], P('dp'), may hold values from 0 to 3, all different within a row; in each aligned block of 8 rows (0 to 7, 8 to 15, ...) at most 8 rows name the same one
- route_weights: float32 [64, 2], P('dp'), may hold values from 0.2 to 1
- norm_gains: float32 [4, 4096], P('branch'), may hold values from 0.25 to 1.75
- keyval_weights: bfloat16 [4, 4096, 2048], P('branch', 'dp'), may hold values from -0.09375 to 0.09375
- expert_gate: bfloat16 [4, 4096, 8192], P('branch', None, 'dp'), may hold values from -0.09375 to 0.09375
- expert_up: bfloat16 [4, 4096, 8192], P('branch', None, 'dp'), may hold values from -0.09375 to 0.09375
- expert_down: bfloat16 [4, 8192, 4096], P('branch', None, 'dp'), may hold values from -0.0625 to 0.0625
Outputs:
- mixed: bfloat16 [64, 4096], P('dp')
- merged_keyval: bfloat16 [4096, 2048], P('dp', 'branch')
Inputs may be any that keep to these rules, and one draw needn't show every extreme that they name: `routes`: each token names 2 different experts. Among the 8 tokens of one dp index at most 8 name one expert, a bound that some block reaches.
All inputs are finite; a program needn't handle non-finite values.
Results may differ from a plain program's by a relative error of at most 0.013.
Values may be sent and summed in bfloat16 or wider, within the bound.
A program may use at most 64 MiB of HBM per device.

v0:
```python
import jax
import jax.numpy as jnp
from jax import lax
from jax.sharding import PartitionSpec as P


def merge_keyval(keyval_weights, branches):
    summed = lax.psum_scatter(
        keyval_weights[0].astype(jnp.float32).astype(jnp.bfloat16),
        "branch",
        scatter_dimension=1,
        tiled=True,
    ).astype(jnp.float32)
    return (summed / branches).astype(jnp.bfloat16)


def normalize(block_rows, gain_avg):
    widened = block_rows.astype(jnp.float32)
    inv_rms = lax.rsqrt(jnp.mean(widened * widened, axis=1, keepdims=True) + 1e-05)
    return (widened * inv_rms * gain_avg[None, :]).astype(jnp.bfloat16)


def local(
    tokens, routes, route_weights, norm_gains, keyval_weights, expert_gate, expert_up, expert_down
):
    branches = lax.axis_size("branch")
    expert = lax.axis_index("branch")
    tok_count = tokens.shape[0]
    capacity = min(tok_count, 4 * tok_count // branches)
    merged_keyval = merge_keyval(keyval_weights, branches)
    gain_avg = lax.psum(norm_gains[0], "branch") / branches
    matched = routes == expert
    chosen = jnp.any(matched, axis=1)
    weight_share = jnp.sum(jnp.where(matched, route_weights, jnp.zeros_like(route_weights)), axis=1)
    slot_index = jnp.cumsum(chosen.astype(jnp.int32)) - 1
    picks = (
        (slot_index[None, :] == jnp.arange(capacity, dtype=jnp.int32)[:, None]) & chosen[None, :]
    ).astype(jnp.bfloat16)
    source_rows = normalize(tokens, gain_avg)
    packed = jnp.dot(picks, source_rows, preferred_element_type=jnp.float32).astype(jnp.bfloat16)
    block_rows = lax.all_gather(packed, "dp", axis=0, tiled=True)
    gate_part = jnp.dot(block_rows, expert_gate[0], preferred_element_type=jnp.float32)
    up_part = jnp.dot(block_rows, expert_up[0], preferred_element_type=jnp.float32)
    hidden = (jax.nn.silu(gate_part) * up_part).astype(jnp.bfloat16)
    down_rows = expert_down[0]
    result_cols = lax.dot_general(
        down_rows,
        lax.all_gather(hidden, "dp", axis=1, tiled=True),
        (((0,), (1,)), ((), ())),
        preferred_element_type=jnp.float32,
    ).astype(jnp.bfloat16)
    own_slots = lax.all_to_all(result_cols, "dp", split_axis=1, concat_axis=0, tiled=True)
    returned = (
        lax.dot_general(
            picks, own_slots, (((0,), (1,)), ((), ())), preferred_element_type=jnp.float32
        )
        * weight_share[:, None]
    )
    expert_total = lax.psum(returned, "branch")
    mixed = (tokens.astype(jnp.float32) + expert_total).astype(jnp.bfloat16)
    return (mixed, merged_keyval)


def solution(mesh):
    in_specs = (
        P("dp", None),
        P("dp", None),
        P("dp", None),
        P("branch", None),
        P("branch", "dp", None),
        P("branch", None, "dp"),
        P("branch", None, "dp"),
        P("branch", None, "dp"),
    )
    out_specs = (P("dp", None), P("dp", "branch"))
    return jax.shard_map(local, mesh=mesh, in_specs=in_specs, out_specs=out_specs, check_vma=False)
```

profile of v0, /device:TPU:0, one launch (start us, length us, event | category | flops | bytes accessed | tf_op | source)
XLA Modules:
  0.0 173.1 jit_solution(810726054813497123)
XLA Ops:
  7.2 0.0 all-gather.2.cloned.1.call-start
  7.2 0.7 fusion.32
  7.9 0.2 reduce-window.8
  8.1 21.1 %psum.14 = f32[4096]{0:T(1024)S(1)} all-reduce(f32[4096]{0:T(1024)} %bitcast.38), channel_id=1, replica_groups=mesh['branch'=4,'dp'=8] {'branch'}, use_global_device_ids=true, to_apply=%region_3.4 | all-reduce | flops 4096 | bytes 32768 | tf_op jit(solution)/shard_map/psum | solution.py:31
  29.2 1.0 fusion.18
  30.2 1.0 convolution_convert_fusion
  31.3 10.1 %all_gather.6 = bf16[64,4096]{1,0:T(8,128)(2,1)S(1)} all-gather(bf16[8,4096]{1,0:T(8,128)(2,1)S(1)} %convolution_convert_fusion), channel_id=1, replica_groups=mesh['branch'=4,'dp'=8] {'dp'}, dimensions={0}, use_global_device_ids=true | all-gather | bytes 589824 | tf_op jit(solution)/shard_map/all_gather | solution.py:41
  41.4 5.1 %fusion.4 = f32[64,1024]{1,0:T(8,128)S(1)} fusion(bf16[64,4096]{1,0:T(8,128)(2,1)S(1)} %all_gather.6, bf16[1,4096,1024]{2,1,0:T(8,128)(2,1)} %param.13), kind=kOutput, calls=%fused_computation.4 | convolution fusion | flops 536870912 | bytes 9175040 | tf_op jit(solution)/shard_map/dot_general | solution.py:42
  46.6 2.3 %fusion.9 = bf16[64,1024]{1,0:T(8,128)(2,1)} fusion(bf16[64,4096]{1,0:T(8,128)(2,1)S(1)} %all_gather.6, bf16[1,4096,1024]{2,1,0:T(8,128)(2,1)S(1)} %bitcast.35, f32[64,1024]{1,0:T(8,128)S(1)} %fusion.4), kind=kOutput, calls=%fused_computation.9 | convolution fusion | flops 537264128 | bytes 9306112 | tf_op jit(solution)/shard_map/dot_general | solution.py:43
  48.8 0.0 all-gather.2.cloned.1.call-update
  48.9 0.0 copy-start.2
  48.9 20.9 %all-gather.2.cloned.1.call-done = bf16[64,8192]{1,0:T(8,128)(2,1)} async-done(((bf16[64,1024]{1,0:T(8,128)(2,1)}), bf16[64,8192]{1,0:T(8,128)(2,1)}) %all-gather.2.cloned.1.call-update) | async-done | bytes 1048592 | tf_op jit(solution)/shard_map/all_gather | solution.py:48
  69.8 5.9 %fusion.15 = bf16[512,8,8]{0,2,1:T(8,128)(2,1)} fusion(bf16[64,8192]{1,0:T(8,128)(2,1)} %all-gather.2.cloned.1.call-done, bf16[1,8192,512]{2,1,0:T(8,128)(2,1)} %param.15), kind=kOutput, calls=%fused_computation.11 | convolution fusion | flops 536903680 | bytes 9502720 | tf_op jit(solution)/shard_map/dot_general | solution.py:46
  75.7 3.4 %all-to-all-start = ((bf16[512,8,8]{0,2,1:T(8,128)(2,1)}), bf16[512,8,8]{0,2,1:T(8,128)(2,1)S(1)}, u32[]{:S(2)}, u32[]{:S(2)}) async-start(bf16[512,8,8]{0,2,1:T(8,128)(2,1)} %fusion.15), calls=%async_computation | async-start | bytes 131072 | tf_op jit(solution)/shard_map/all_to_all | solution.py:52
  79.1 0.0 all-reduce.2.cloned.1.call-start
  79.2 4.9 %all-to-all-done = bf16[512,8,8]{0,2,1:T(8,128)(2,1)S(1)} async-done(((bf16[512,8,8]{0,2,1:T(8,128)(2,1)}), bf16[512,8,8]{0,2,1:T(8,128)(2,1)S(1)}, u32[]{:S(2)}, u32[]{:S(2)}) %all-to-all-start) | async-done | bytes 65568 | tf_op jit(solution)/shard_map/all_to_all | solution.py:52
  84.0 0.9 convolution_multiply_fusion
  84.9 0.0 all-reduce.2.cloned.1.call-update
  84.9 0.0 reduce-scatter.2.cloned.1.call-start
  85.0 0.7 reduce-scatter.2.cloned.1.call-update
  85.7 33.0 %all-reduce.2.cloned.1.call-done = f32[8,4096]{1,0:T(8,128)} async-done(((f32[8,4096]{1,0:T(8,128)}), f32[8,4096]{1,0:T(8,128)}) %all-reduce.2.cloned.1.call-update) | async-done | bytes 131088 | tf_op jit(solution)/shard_map/psum | solution.py:59
  118.7 1.5 fusion.21
  120.2 44.4 %reduce-scatter.2.cloned.1.call-done = bf16[512,512]{1,0:T(8,128)(2,1)} async-done(((bf16[512,2048]{1,0:T(8,128)(2,1)}), bf16[512,512]{1,0:T(8,128)(2,1)}) %reduce-scatter.2.cloned.1.call-update) | async-done | bytes 524304 | tf_op jit(solution)/shard_map/reduce_scatter | solution.py:8
  164.6 1.9 %multiply_convert_fusion = bf16[512,512]{1,0:T(8,128)(2,1)} fusion(bf16[512,512]{1,0:T(8,128)(2,1)} %reduce-scatter.2.cloned.1.call-done), kind=kLoop, calls=%fused_computation.12 | loop fusion | flops 786432 | bytes 1048576 | tf_op jit(solution)/shard_map/convert_element_type | solution.py:14
  (15 shorter events, 0.1 us)
Async XLA Ops:
  7.2 62.7 %all-gather.2.cloned.1.call-start = ((), (), s32[]{:S(2)}) async-start(), calls=%async_computation.2 | async-start | bytes 1179648 | tf_op jit(solution)/shard_map/all_gather | solution.py:48
  31.3 15.3 %slice-start = ((s8[8388608]{0:T(1024)(128)(4,1)}), s8[4194304]{0:T(1024)(128)(4,1)S(1)}, s32[]{:S(2)}) async-start(s8[8388608]{0:T(1024)(128)(4,1)} %bitcast.34), calls=%async_computation.5 | async-start | bytes 8388608
  41.4 5.1 %slice-start.1 = ((s8[8388608]{0:T(1024)(128)(4,1)}), s8[4194304]{0:T(1024)(128)(4,1)S(1)}, s32[]{:S(2)}) async-start(s8[8388608]{0:T(1024)(128)(4,1)} %bitcast.34), calls=%async_computation.6 | async-start | bytes 8388608
  48.9 30.3 %copy-start.1 = (s32[8,2]{0,1:T(2,128)S(1)}, s32[8,2]{0,1:T(2,128)}, u32[]{:S(2)}) copy-start(s32[8,2]{0,1:T(2,128)} %param.9) | copy-start | bytes 196
  48.9 30.3 %copy-start.2 = (f32[8,2]{0,1:T(2,128)S(1)}, f32[8,2]{0,1:T(2,128)}, u32[]{:S(2)}) copy-start(f32[8,2]{0,1:T(2,128)} %param.10) | copy-start | bytes 196
  48.9 69.8 %copy-start = (bf16[8,4096]{1,0:T(8,128)(2,1)S(1)}, bf16[8,4096]{1,0:T(8,128)(2,1)}, u32[]{:S(2)}) copy-start(bf16[8,4096]{1,0:T(8,128)(2,1)} %param.8) | copy-start | bytes 196612
  75.7 8.3 %all-to-all-start = ((bf16[512,8,8]{0,2,1:T(8,128)(2,1)}), bf16[512,8,8]{0,2,1:T(8,128)(2,1)S(1)}, u32[]{:S(2)}, u32[]{:S(2)}) async-start(bf16[512,8,8]{0,2,1:T(8,128)(2,1)} %fusion.15), calls=%async_computation | async-start | bytes 131072 | tf_op jit(solution)/shard_map/all_to_all | solution.py:52
  79.1 39.6 %all-reduce.2.cloned.1.call-start = ((), (), s32[]{:S(2)}) async-start(), calls=%async_computation.3 | async-start | bytes 262144 | tf_op jit(solution)/shard_map/psum | solution.py:59
  84.9 79.7 %reduce-scatter.2.cloned.1.call-start = ((), (), s32[]{:S(2)}) async-start(), calls=%async_computation.4 | async-start | bytes 2621440 | tf_op jit(solution)/shard_map/reduce_scatter | solution.py:8
Sparse Core Ops, SparseCore 0:
  49.0 20.7 all-gather.1
  85.0 33.5 all-reduce.1
  121.1 43.4 reduce-scatter.1
where the time goes:
time: 174 us; the launch traced here: 173 us
  waiting for transfers between devices  104 us (60%)
  blocking collectives  31.3 us (18%)
  matrix products  15.2 us (9%)
  between operations  13.8 us (8%)
  other arithmetic  5.39 us (3%)
  starting transfers between devices  3.47 us (2%)
    reduce_scatter x1, waiting for transfers between devices, merge_keyval(): lax.psum_scatter(keyval_weights[0].astype(jnp.float32).astype(jnp.bfloat1...  44.4 us
    psum x1, waiting for transfers between devices, local(): expert_total = lax.psum(returned, 'branch')  33 us
    psum x1, blocking collectives, local(): gain_avg = lax.psum(norm_gains[0], 'branch') / branches  21.1 us
    all_gather x1, waiting for transfers between devices, local(): lax.all_gather(hidden, 'dp', axis=1, tiled=True)  20.9 us
    all_gather x1, blocking collectives, local(): block_rows = lax.all_gather(packed, 'dp', axis=0, tiled=True)  10.1 us
    dot_general x1, matrix products, local(): lax.dot_general(down_rows, lax.all_gather(hidden, 'dp', axis=1, tiled=Tru...  5.91 us
    dot_general x1, matrix products, local(): jnp.dot(block_rows, expert_gate[0], preferred_element_type=jnp.float32)  5.11 us
    all_to_all x1, waiting for transfers between devices, local(): lax.all_to_all(result_cols, 'dp', split_axis=1, concat_axis=0, tiled=True)  4.86 us
  transfers between devices with their start and end apart: 4, of which 4 were waited for; matrix products, arithmetic and copies ran while one was open for 1% of the time, Pallas kernels for 0%

commit v1 on v0

v1 whole, which is shorter than its diff:
```python
import functools

import jax
import jax.numpy as jnp
from jax import lax
from jax.experimental import pallas as pl
from jax.experimental.pallas import tpu as pltpu
from jax.sharding import PartitionSpec as P

MESH = pl.DeviceIdType.MESH
CHUNKS = 2


def kernel(
    B,
    N,
    tokens,
    routes,
    route_weights,
    gains,
    keyval,
    gate,
    up,
    down,
    moe_out,
    kv_out,
    tg,
    gg,
    normed,
    wg,
    wu,
    wd,
    kv,
    flow,
    hid,
    acc,
    rs,
    ret,
    part,
    tok_s,
    tok_r,
    gain_s,
    gain_r,
    hid_s,
    hid_r,
    ret_s,
    ret_r,
    part_s,
    part_r,
    kv_s,
    kv_r,
    wg_sem,
    wu_sem,
    wd_sem,
    kv_sem,
):
    b, me = lax.axis_index("branch"), lax.axis_index("dp")
    T, D = tokens.shape
    R = N * T
    C, _, ct = hid.shape[1], hid.shape[2], hid.shape[3]
    rows, bw = kv_out.shape
    crows = rows // CHUNKS
    F = C * ct

    def dp_peer(k):
        return lax.rem(me + k, N)

    def br_peer(k):
        return lax.rem(b + k, B)

    load_kv = pltpu.make_async_copy(keyval.at[0], kv, kv_sem)
    load_kv.start()
    loads = []
    for c in range(C):
        cols = pl.ds(c * ct, ct)
        one = pltpu.make_async_copy(gate.at[0, :, cols], wg.at[c], wg_sem.at[c])
        two = pltpu.make_async_copy(up.at[0, :, cols], wu.at[c], wu_sem.at[c])
        one.start()
        two.start()
        loads.append((one, two))
    load_wd = pltpu.make_async_copy(down.at[0], wd, wd_sem)
    load_wd.start()

    barrier = pltpu.get_barrier_semaphore()

    @pl.loop(1, N)
    def _(k):
        pl.semaphore_signal(barrier, inc=1, device_id={"dp": dp_peer(k)}, device_id_type=MESH)

    @pl.loop(1, B)
    def _(k):
        pl.semaphore_signal(barrier, inc=1, device_id={"branch": br_peer(k)}, device_id_type=MESH)

    tg[me] = tokens[...]
    gg[b] = gains[...]
    pl.semaphore_wait(barrier, N - 1 + B - 1)

    def dp_copy(src, dst, ss, rsm, peer):
        return pltpu.make_async_remote_copy(
            src_ref=src, dst_ref=dst, send_sem=ss, recv_sem=rsm,
            device_id={"dp": peer}, device_id_type=MESH,
        )

    def br_copy(src, dst, ss, rsm, peer):
        return pltpu.make_async_remote_copy(
            src_ref=src, dst_ref=dst, send_sem=ss, recv_sem=rsm,
            device_id={"branch": peer}, device_id_type=MESH,
        )

    def gain_copy(slot, peer):
        return br_copy(gg.at[slot], gg.at[slot], gain_s.at[peer], gain_r.at[slot], peer)

    def tok_copy(slot, peer):
        return dp_copy(tg.at[slot], tg.at[slot], tok_s.at[peer], tok_r.at[slot], peer)

    @pl.loop(1, B)
    def _(k):
        gain_copy(b, br_peer(k)).start()

    @pl.loop(1, N)
    def _(k):
        tok_copy(me, dp_peer(k)).start()

    steps = CHUNKS * (B - 1)
    place = (b, B - 1 - b)

    def target(way, s):
        far = B - 1 - s // CHUNKS
        return far, (far if way == 0 else B - 1 - far)

    def kv_copy(way, d, c):
        to = jnp.clip(b + 1 if way == 0 else b - 1, 0, B - 1)
        slot = flow.at[way, d, c]
        return br_copy(slot, slot, kv_s.at[way, d, c], kv_r.at[way, d, c], to)

    def own(d, c):
        return kv[pl.ds(c * crows, crows), pl.ds(pl.multiple_of(d * bw, bw), bw)]

    def step(way, s):
        at = place[way]
        far, d = target(way, s)
        c = lax.rem(s, CHUNKS)

        @pl.when((s >= 0) & (s < steps) & (far > at))
        def _():
            mine = kv[
                pl.ds(pl.multiple_of(c * crows, crows), crows),
                pl.ds(pl.multiple_of(d * bw, bw), bw),
            ]

            @pl.when(at == 0)
            def _():
                flow[way, d, c] = mine

            @pl.when(at > 0)
            def _():
                kv_copy(way, d, c).wait_recv()
                flow[way, d, c] = (
                    flow[way, d, c].astype(jnp.float32) + mine.astype(jnp.float32)
                ).astype(jnp.bfloat16)

            kv_copy(way, d, c).start()

    def sent(way, s):
        far, d = target(way, s)
        c = lax.rem(s, CHUNKS)

        @pl.when((s >= 0) & (s < steps) & (far > place[way]))
        def _():
            kv_copy(way, d, c).wait_send()

    def slot(p):
        for way in range(2):
            s = jnp.where(place[way] == 0, p + 1, p - place[way])
            sent(way, s - 2)
            step(way, s)

    load_kv.wait()
    slot(jnp.int32(-1))
    slot(jnp.int32(0))

    @pl.loop(1, B)
    def _(k):
        gain_copy(br_peer(k), br_peer(k)).wait_recv()

    gain = gg[0]
    for e in range(1, B):
        gain = gain + gg[e]
    gain = gain / B
    gg_avg = gain

    @pl.loop(1, N)
    def _(k):
        tok_copy(dp_peer(k), dp_peer(k)).wait_recv()

    pair = 2

    @pl.loop(0, N // pair)
    def _(i):
        x = jnp.concatenate([tg[i * pair + q].astype(jnp.float32) for q in range(pair)], axis=0)
        inv = lax.rsqrt(jnp.mean(x * x, axis=1, keepdims=True) + 1e-05)
        normed[pl.ds(pl.multiple_of(i * pair * T, pair * T), pair * T), :] = (
            x * inv * gg_avg
        ).astype(jnp.bfloat16)

    def hid_copy(c, slot_, peer):
        return dp_copy(
            hid.at[slot_, c], hid.at[slot_, c], hid_s.at[c, peer], hid_r.at[c, slot_], peer
        )

    for c in range(C):
        loads[c][0].wait()
        loads[c][1].wait()
        x = normed[...]
        g = jnp.dot(x, wg[c], preferred_element_type=jnp.float32)
        u = jnp.dot(x, wu[c], preferred_element_type=jnp.float32)
        hid[me, c] = (g / (1.0 + jnp.exp(-g)) * u).astype(jnp.bfloat16)

        @pl.loop(1, N)
        def _(k, c=c):
            hid_copy(c, me, dp_peer(k)).start()

    slot(jnp.int32(1))

    load_wd.wait()
    acc[...] = jnp.zeros_like(acc)
    for c in range(C):

        @pl.loop(0, N)
        def _(k, c=c):
            j = dp_peer(k)

            @pl.when(k > 0)
            def _():
                hid_copy(c, j, j).wait_recv()

            acc[...] += jnp.dot(
                hid[j, c],
                wd[pl.ds(pl.multiple_of(j * F + c * ct, ct), ct), :],
                preferred_element_type=jnp.float32,
            )

    slot(jnp.int32(2))

    def ret_copy(i, peer, from_):
        return dp_copy(rs.at[i], ret.at[from_], ret_s.at[i], ret_r.at[from_], peer)

    @pl.loop(0, N)
    def _(i):
        rs[i] = acc[pl.ds(pl.multiple_of(i * T, T), T), :].astype(jnp.bfloat16)

    @pl.loop(1, N)
    def _(k):
        ret_copy(dp_peer(k), dp_peer(k), me).start()

    ret[me] = rs[me]
    weight = jnp.sum(
        jnp.where(routes[...] == b, route_weights[...], 0.0), axis=1, keepdims=True
    )

    @pl.loop(0, N)
    def _(k):
        j = dp_peer(k)

        @pl.when(k > 0)
        def _():
            ret_copy(j, j, j).wait_recv()

        part[b, j] = (ret[j].astype(jnp.float32) * weight).astype(jnp.bfloat16)

    def part_copy(e, peer):
        return br_copy(part.at[e], part.at[e], part_s.at[peer], part_r.at[e], peer)

    @pl.loop(1, B)
    def _(k):
        part_copy(b, br_peer(k)).start()

    slot(jnp.int32(3))

    @pl.loop(1, B)
    def _(k):
        part_copy(br_peer(k), br_peer(k)).wait_recv()

    @pl.loop(0, N)
    def _(j):
        total = part[0, j].astype(jnp.float32)
        for e in range(1, B):
            total = total + part[e, j].astype(jnp.float32)
        moe_out[j] = total

    @pl.loop(4, steps + B)
    def _(p):
        slot(p)

    for way in range(2):

        @pl.when(place[way] == 0)
        def _(way=way):
            flow[way, b] = jnp.zeros_like(flow[way, b])

        @pl.when(place[way] > 0)
        def _(way=way):
            for c in range(CHUNKS):
                kv_copy(way, b, c).wait_recv()

    for c in range(CHUNKS):
        total = (
            own(b, c).astype(jnp.float32)
            + flow[0, b, c].astype(jnp.float32)
            + flow[1, b, c].astype(jnp.float32)
        )
        kv_out[pl.ds(c * crows, crows), :] = (total / B).astype(jnp.bfloat16)

    for way in range(2):
        last = jnp.where(place[way] == 0, steps + B, steps + B - 1 - place[way])

        @pl.loop(0, steps)
        def _(s, way=way, last=last):
            @pl.when(s > last - 2)
            def _():
                sent(way, s)

    @pl.loop(1, B)
    def _(k):
        gain_copy(b, br_peer(k)).wait_send()
        part_copy(b, br_peer(k)).wait_send()

    @pl.loop(1, N)
    def _(k):
        tok_copy(me, dp_peer(k)).wait_send()
        ret_copy(dp_peer(k), dp_peer(k), me).wait_send()
        for c in range(C):
            hid_copy(c, me, dp_peer(k)).wait_send()


def local(tokens, routes, route_weights, norm_gains, keyval, gate, up, down):
    B, N = lax.axis_size("branch"), lax.axis_size("dp")
    T, D = tokens.shape
    F = gate.shape[2]
    ct = min(256, F)
    C = F // ct
    rows, wide = keyval.shape[1:]
    bw = wide // B
    H, bc = down.shape[1:]
    bf, f32 = jnp.bfloat16, jnp.float32
    dma = pltpu.SemaphoreType.DMA
    vmem, anys = pl.BlockSpec(memory_space=pltpu.VMEM), pl.BlockSpec(memory_space=pl.ANY)
    moe, merged = pl.pallas_call(
        functools.partial(kernel, B, N),
        out_shape=(
            jax.ShapeDtypeStruct((N, T, bc), f32),
            jax.ShapeDtypeStruct((rows, bw), bf),
        ),
        in_specs=[vmem] * 4 + [anys] * 4,
        out_specs=(vmem, vmem),
        scratch_shapes=[
            pltpu.VMEM((N, T, D), bf),
            pltpu.VMEM((B, 1, D), f32),
            pltpu.VMEM((N * T, D), bf),
            pltpu.VMEM((C, D, ct), bf),
            pltpu.VMEM((C, D, ct), bf),
            pltpu.VMEM((H, bc), bf),
            pltpu.VMEM((rows, wide), bf),
            pltpu.VMEM((2, B, CHUNKS, rows // CHUNKS, bw), bf),
            pltpu.VMEM((N, C, N * T, ct), bf),
            pltpu.VMEM((N * T, bc), f32),
            pltpu.VMEM((N, T, bc), bf),
            pltpu.VMEM((N, T, bc), bf),
            pltpu.VMEM((B, N, T, bc), bf),
            dma((N,)),
            dma((N,)),
            dma((B,)),
            dma((B,)),
            dma((C, N)),
            dma((C, N)),
            dma((N,)),
            dma((N,)),
            dma((B,)),
            dma((B,)),
            dma((2, B, CHUNKS)),
            dma((2, B, CHUNKS)),
            dma((C,)),
            dma((C,)),
            dma,
            dma,
        ],
        compiler_params=pltpu.CompilerParams(
            collective_id=0, has_side_effects=True, vmem_limit_bytes=56 * 2**20
        ),
    )(tokens, routes, route_weights, norm_gains, keyval, gate, up, down)
    moe = jnp.transpose(moe, (1, 0, 2)).reshape(T, D)
    return (tokens.astype(f32) + moe).astype(bf), merged


def solution(mesh):
    in_specs = (
        P("dp", None),
        P("dp", None),
        P("dp", None),
        P("branch", None),
        P("branch", "dp", None),
        P("branch", None, "dp"),
        P("branch", None, "dp"),
        P("branch", None, "dp"),
    )
    out_specs = (P("dp", None), P("dp", "branch"))
    return jax.shard_map(local, mesh=mesh, in_specs=in_specs, out_specs=out_specs, check_vma=False)
```

time: 174 us -> 61.8 us (0.36)
  waiting for transfers between devices: 104 us -> 0 us
  Pallas kernels: 0 us -> 53.9 us
  blocking collectives: 31.3 us -> 0 us
  matrix products: 15.2 us -> 0 us
  between operations: 13.8 us -> 0.65 us
  local copies, waits for them, and re-layouts: 0.03 us -> 4.56 us
  other arithmetic: 5.39 us -> 1.55 us
  starting transfers between devices: 3.47 us -> 0 us
    pallas_call x0 -> x1, Pallas kernels: none -> 53.9 us  [local(): pl.pallas_call(functools.partial(kernel, B, N), out_shape=(jax.ShapeDtype...]
    reduce_scatter x1 -> x0, waiting for transfers between devices: 44.4 us -> none  [merge_keyval(): lax.psum_scatter(keyval_weights[0].astype(jnp.float32).astype(jnp.bfloat1...]
    psum x1 -> x0, waiting for transfers between devices: 33 us -> none  [local(): expert_total = lax.psum(returned, 'branch')]
    psum x1 -> x0, blocking collectives: 21.1 us -> none  [local(): gain_avg = lax.psum(norm_gains[0], 'branch') / branches]
    all_gather x1 -> x0, waiting for transfers between devices: 20.9 us -> none  [local(): lax.all_gather(hidden, 'dp', axis=1, tiled=True)]
    dot_general x5 -> x0, matrix products: 15.2 us -> none  [the longest x1 5.91 us: local(): lax.dot_general(down_rows, lax.all_gather(hidden, 'dp', axis=1, tiled=Tru...]
    all_gather x1 -> x0, blocking collectives: 10.1 us -> none  [local(): block_rows = lax.all_gather(packed, 'dp', axis=0, tiled=True)]
    all_to_all x1 -> x0, waiting for transfers between devices: 4.86 us -> none  [local(): lax.all_to_all(result_cols, 'dp', split_axis=1, concat_axis=0, tiled=True)]
  transfers between devices with their start and end apart: 4 -> 0, of which waited for: 4 -> 0; matrix products, arithmetic and copies ran while one was open for 1% -> 0% of each run, Pallas kernels for 0% -> 0%
where the time goes in v1:
time: 61.8 us; the launch traced here: 60.7 us
  Pallas kernels  53.9 us (87%)
  local copies, waits for them, and re-layouts  4.56 us (7%)
  other arithmetic  1.55 us (3%)
  between operations  0.65 us (1%)
    pallas_call x1, Pallas kernels, local(): pl.pallas_call(functools.partial(kernel, B, N), out_shape=(jax.ShapeDtype...  53.9 us
    unnamed x5, local copies, waits for them, and re-layouts  4.56 us
    convert_element_type x1, other arithmetic, local(): return ((tokens.astype(f32) + moe).astype(bf), merged)  1.55 us

profile of v1, /device:TPU:0, one launch (start us, length us, event | category | flops | bytes accessed | tf_op | source)
XLA Modules:
  0.0 60.7 jit_solution(1561321835962857829)
XLA Ops:
  0.6 1.3 %copy.10.routes = s32[8,2]{1,0:T(8,128)} copy(s32[8,2]{0,1:T(2,128)} %param.9) | data formatting | bytes 128 | tf_op args[1]
  2.0 1.3 %copy.11.route_weights = f32[8,2]{1,0:T(8,128)} copy(f32[8,2]{0,1:T(2,128)} %param.10) | data formatting | bytes 128 | tf_op args[2]
  3.3 0.0 copy-start
  3.3 53.9 %shard_map.95 = (f32[8,8,512]{2,1,0:T(8,128)}, bf16[512,512]{1,0:T(8,128)(2,1)}) custom-call(bf16[8,4096]{1,0:T(8,128)(2,1)} %tokens.1, s32[8,2]{1,0:T(8,128)} %copy.10.routes, f32[8,2]{1,0:T(8,128)} %copy.11.route_weights, f32[1,4096]{1,0:T(1,128)} %gains.1, bf16[1,512,2048]{2,1,0:T(8,128)(2,1)} %keyval.1, bf16[1,4096,1024]{2,1,0:T(8,128)(2,1)} %gate.1, ...), custom_call_target="tpu_custom_call" | custom-call | tf_op jit(solution)/shard_map/pallas_call | solution.py:348
  57.3 0.0 copy-done
  57.3 1.5 %add_convert_fusion = bf16[8,4096]{1,0:T(8,128)(2,1)} fusion(f32[8,4096]{1,0:T(8,128)} %bitcast.3, bf16[8,4096]{1,0:T(8,128)(2,1)S(1)} %copy-done), kind=kLoop, calls=%fused_computation | loop fusion | flops 98304 | bytes 262144 | tf_op jit(solution)/shard_map/convert_element_type | solution.py:392
  58.8 1.9 %copy.13 = bf16[512,512]{1,0:T(8,128)(2,1)} copy(bf16[512,512]{1,0:T(8,128)(2,1)} %get-tuple-element.9) | data formatting | bytes 1048576
Async XLA Ops:
  3.3 53.9 %copy-start = (bf16[8,4096]{1,0:T(8,128)(2,1)S(1)}, bf16[8,4096]{1,0:T(8,128)(2,1)}, u32[]{:S(2)}) copy-start(bf16[8,4096]{1,0:T(8,128)(2,1)} %tokens.1) | copy-start | bytes 196612

commit v2 on v1

--- a/solution.py
+++ b/solution.py
@@ -70,6 +70,46 @@
 
     load_kv = pltpu.make_async_copy(keyval.at[0], kv, kv_sem)
     load_kv.start()
+    barrier = pltpu.get_barrier_semaphore()
+
+    @pl.loop(1, N)
+    def _(k):
+        pl.semaphore_signal(barrier, inc=1, device_id={"dp": dp_peer(k)}, device_id_type=MESH)
+
+    @pl.loop(1, B)
+    def _(k):
+        pl.semaphore_signal(barrier, inc=1, device_id={"branch": br_peer(k)}, device_id_type=MESH)
+
+    tg[me] = tokens[...]
+    gg[b] = gains[...]
+    pl.semaphore_wait(barrier, N - 1 + B - 1)
+
+    def dp_copy(src, dst, ss, rsm, peer):
+        return pltpu.make_async_remote_copy(
+            src_ref=src, dst_ref=dst, send_sem=ss, recv_sem=rsm,
+            device_id={"dp": peer}, device_id_type=MESH,
+        )
+
+    def br_copy(src, dst, ss, rsm, peer):
+        return pltpu.make_async_remote_copy(
+            src_ref=src, dst_ref=dst, send_sem=ss, recv_sem=rsm,
+            device_id={"branch": peer}, device_id_type=MESH,
+        )
+
+    def gain_copy(slot, peer):
+        return br_copy(gg.at[slot], gg.at[slot], gain_s.at[peer], gain_r.at[slot], peer)
+
+    def tok_copy(slot, peer):
+        return dp_copy(tg.at[slot], tg.at[slot], tok_s.at[peer], tok_r.at[slot], peer)
+
+    @pl.loop(1, B)
+    def _(k):
+        gain_copy(b, br_peer(k)).start()
+
+    @pl.loop(1, N)
+    def _(k):
+        tok_copy(me, dp_peer(k)).start()
+
     loads = []
     for c in range(C):
         cols = pl.ds(c * ct, ct)
@@ -81,46 +121,6 @@
     load_wd = pltpu.make_async_copy(down.at[0], wd, wd_sem)
     load_wd.start()
 
-    barrier = pltpu.get_barrier_semaphore()
-
-    @pl.loop(1, N)
-    def _(k):
-        pl.semaphore_signal(barrier, inc=1, device_id={"dp": dp_peer(k)}, device_id_type=MESH)
-
-    @pl.loop(1, B)
-    def _(k):
-        pl.semaphore_signal(barrier, inc=1, device_id={"branch": br_peer(k)}, device_id_type=MESH)
-
-    tg[me] = tokens[...]
-    gg[b] = gains[...]
-    pl.semaphore_wait(barrier, N - 1 + B - 1)
-
-    def dp_copy(src, dst, ss, rsm, peer):
-        return pltpu.make_async_remote_copy(
-            src_ref=src, dst_ref=dst, send_sem=ss, recv_sem=rsm,
-            device_id={"dp": peer}, device_id_type=MESH,
-        )
-
-    def br_copy(src, dst, ss, rsm, peer):
-        return pltpu.make_async_remote_copy(
-            src_ref=src, dst_ref=dst, send_sem=ss, recv_sem=rsm,
-            device_id={"branch": peer}, device_id_type=MESH,
-        )
-
-    def gain_copy(slot, peer):
-        return br_copy(gg.at[slot], gg.at[slot], gain_s.at[peer], gain_r.at[slot], peer)
-
-    def tok_copy(slot, peer):
-        return dp_copy(tg.at[slot], tg.at[slot], tok_s.at[peer], tok_r.at[slot], peer)
-
-    @pl.loop(1, B)
-    def _(k):
-        gain_copy(b, br_peer(k)).start()
-
-    @pl.loop(1, N)
-    def _(k):
-        tok_copy(me, dp_peer(k)).start()
-
     steps = CHUNKS * (B - 1)
     place = (b, B - 1 - b)
 
@@ -220,7 +220,10 @@
         def _(k, c=c):
             hid_copy(c, me, dp_peer(k)).start()
 
-    slot(jnp.int32(1))
+        if c == 0:
+            slot(jnp.int32(1))
+        if c == C - 1:
+            slot(jnp.int32(2))
 
     load_wd.wait()
     acc[...] = jnp.zeros_like(acc)
@@ -240,7 +243,10 @@
                 preferred_element_type=jnp.float32,
             )
 
-    slot(jnp.int32(2))
+        if c == 0:
+            slot(jnp.int32(3))
+        if c == C - 1:
+            slot(jnp.int32(4))
 
     def ret_copy(i, peer, from_):
         return dp_copy(rs.at[i], ret.at[from_], ret_s.at[i], ret_r.at[from_], peer)
@@ -254,9 +260,11 @@
         ret_copy(dp_peer(k), dp_peer(k), me).start()
 
     ret[me] = rs[me]
-    weight = jnp.sum(
-        jnp.where(routes[...] == b, route_weights[...], 0.0), axis=1, keepdims=True
+    row = jnp.sum(jnp.where(routes[...] == b, route_weights[...], 0.0), axis=0, keepdims=True)
+    diagonal = lax.broadcasted_iota(jnp.int32, (T, T), 0) == lax.broadcasted_iota(
+        jnp.int32, (T, T), 1
     )
+    weight = jnp.sum(jnp.where(diagonal, row, 0.0), axis=1, keepdims=True)
 
     @pl.loop(0, N)
     def _(k):
@@ -274,8 +282,6 @@
     @pl.loop(1, B)
     def _(k):
         part_copy(b, br_peer(k)).start()
-
-    slot(jnp.int32(3))
 
     @pl.loop(1, B)
     def _(k):
@@ -288,7 +294,7 @@
             total = total + part[e, j].astype(jnp.float32)
         moe_out[j] = total
 
-    @pl.loop(4, steps + B)
+    @pl.loop(5, steps + B)
     def _(p):
         slot(p)
 
@@ -387,7 +393,7 @@
         compiler_params=pltpu.CompilerParams(
             collective_id=0, has_side_effects=True, vmem_limit_bytes=56 * 2**20
         ),
-    )(tokens, routes, route_weights, norm_gains, keyval, gate, up, down)
+    )(tokens, routes.T, route_weights.T, norm_gains, keyval, gate, up, down)
     moe = jnp.transpose(moe, (1, 0, 2)).reshape(T, D)
     return (tokens.astype(f32) + moe).astype(bf), merged
 

time: 61.8 us -> 53.4 us (0.86); the launches traced: 60.7 us -> 53.2 us
  Pallas kernels: 53.9 us -> 49.1 us
  local copies, waits for them, and re-layouts: 4.56 us -> 1.87 us
    pallas_call x1, Pallas kernels: 53.9 us -> 49.1 us  [local(): pl.pallas_call(functools.partial(kernel, B, N), out_shape=(jax.ShapeDtype...]
    unnamed x5 -> x3, local copies, waits for them, and re-layouts: 4.56 us -> 1.87 us
where the time goes in v2:
time: 53.4 us; the launch traced here: 53.2 us
  Pallas kernels  49.1 us (92%)
  local copies, waits for them, and re-layouts  1.87 us (4%)
  other arithmetic  1.55 us (3%)
  between operations  0.66 us (1%)
    pallas_call x1, Pallas kernels, local(): pl.pallas_call(functools.partial(kernel, B, N), out_shape=(jax.ShapeDtype...  49.1 us
    unnamed x3, local copies, waits for them, and re-layouts  1.87 us
    convert_element_type x1, other arithmetic, local(): return ((tokens.astype(f32) + moe).astype(bf), merged)  1.55 us

profile of v2, /device:TPU:0, one launch (start us, length us, event | category | flops | bytes accessed | tf_op | source)
XLA Modules:
  0.0 53.2 jit_solution(17143307615630784167)
XLA Ops:
  0.6 0.0 copy-start
  0.6 49.1 %shard_map.95 = (f32[8,8,512]{2,1,0:T(8,128)}, bf16[512,512]{1,0:T(8,128)(2,1)}) custom-call(bf16[8,4096]{1,0:T(8,128)(2,1)} %tokens.1, s32[2,8]{1,0:T(2,128)} %bitcast.6, f32[2,8]{1,0:T(2,128)} %bitcast.7, f32[1,4096]{1,0:T(1,128)} %gains.1, bf16[1,512,2048]{2,1,0:T(8,128)(2,1)} %keyval.1, bf16[1,4096,1024]{2,1,0:T(8,128)(2,1)} %gate.1, ...), custom_call_target="tpu_custom_call" | custom-call | tf_op jit(solution)/shard_map/pallas_call | solution.py:354
  49.8 0.0 copy-done
  49.8 1.5 %add_convert_fusion = bf16[8,4096]{1,0:T(8,128)(2,1)} fusion(f32[8,4096]{1,0:T(8,128)} %bitcast.5, bf16[8,4096]{1,0:T(8,128)(2,1)S(1)} %copy-done), kind=kLoop, calls=%fused_computation | loop fusion | flops 98304 | bytes 262144 | tf_op jit(solution)/shard_map/convert_element_type | solution.py:398
  51.3 1.9 %copy.11 = bf16[512,512]{1,0:T(8,128)(2,1)} copy(bf16[512,512]{1,0:T(8,128)(2,1)} %get-tuple-element.9) | data formatting | bytes 1048576
Async XLA Ops:
  0.6 49.1 %copy-start = (bf16[8,4096]{1,0:T(8,128)(2,1)S(1)}, bf16[8,4096]{1,0:T(8,128)(2,1)}, u32[]{:S(2)}) copy-start(bf16[8,4096]{1,0:T(8,128)(2,1)} %tokens.1) | copy-start | bytes 196612

commit v3 on v2

--- a/solution.py
+++ b/solution.py
@@ -102,13 +102,13 @@
     def tok_copy(slot, peer):
         return dp_copy(tg.at[slot], tg.at[slot], tok_s.at[peer], tok_r.at[slot], peer)
 
+    @pl.loop(1, N)
+    def _(k):
+        tok_copy(me, dp_peer(k)).start()
+
     @pl.loop(1, B)
     def _(k):
         gain_copy(b, br_peer(k)).start()
-
-    @pl.loop(1, N)
-    def _(k):
-        tok_copy(me, dp_peer(k)).start()
 
     loads = []
     for c in range(C):
@@ -189,14 +189,16 @@
     gain = gain / B
     gg_avg = gain
 
-    @pl.loop(1, N)
-    def _(k):
-        tok_copy(dp_peer(k), dp_peer(k)).wait_recv()
-
     pair = 2
 
     @pl.loop(0, N // pair)
     def _(i):
+        for q in range(pair):
+
+            @pl.when(i * pair + q != me)
+            def _(q=q):
+                tok_copy(i * pair + q, i * pair + q).wait_recv()
+
         x = jnp.concatenate([tg[i * pair + q].astype(jnp.float32) for q in range(pair)], axis=0)
         inv = lax.rsqrt(jnp.mean(x * x, axis=1, keepdims=True) + 1e-05)
         normed[pl.ds(pl.multiple_of(i * pair * T, pair * T), pair * T), :] = (
@@ -343,7 +345,7 @@
     B, N = lax.axis_size("branch"), lax.axis_size("dp")
     T, D = tokens.shape
     F = gate.shape[2]
-    ct = min(256, F)
+    ct = min(512, F)
     C = F // ct
     rows, wide = keyval.shape[1:]
     bw = wide // B

time: 53.4 us -> 53.2 us (level)
  no operation moved by 1% of the time
where the time goes in v3:
time: 53.2 us; the launch traced here: 53 us
  Pallas kernels  48.9 us (92%)
  local copies, waits for them, and re-layouts  1.87 us (4%)
  other arithmetic  1.55 us (3%)
  between operations  0.66 us (1%)
    pallas_call x1, Pallas kernels, local(): pl.pallas_call(functools.partial(kernel, B, N), out_shape=(jax.ShapeDtype...  48.9 us
    unnamed x3, local copies, waits for them, and re-layouts  1.87 us
    convert_element_type x1, other arithmetic, local(): return ((tokens.astype(f32) + moe).astype(bf), merged)  1.55 us

profile of v3, /device:TPU:0, one launch (start us, length us, event | category | flops | bytes accessed | tf_op | source)
XLA Modules:
  0.0 53.0 jit_solution(10332789668638056205)
XLA Ops:
  0.6 0.0 copy-start
  0.6 48.9 %shard_map.95 = (f32[8,8,512]{2,1,0:T(8,128)}, bf16[512,512]{1,0:T(8,128)(2,1)}) custom-call(bf16[8,4096]{1,0:T(8,128)(2,1)} %tokens.1, s32[2,8]{1,0:T(2,128)} %bitcast.6, f32[2,8]{1,0:T(2,128)} %bitcast.7, f32[1,4096]{1,0:T(1,128)} %gains.1, bf16[1,512,2048]{2,1,0:T(8,128)(2,1)} %keyval.1, bf16[1,4096,1024]{2,1,0:T(8,128)(2,1)} %gate.1, ...), custom_call_target="tpu_custom_call" | custom-call | tf_op jit(solution)/shard_map/pallas_call | solution.py:356
  49.5 0.0 copy-done
  49.6 1.5 %add_convert_fusion = bf16[8,4096]{1,0:T(8,128)(2,1)} fusion(f32[8,4096]{1,0:T(8,128)} %bitcast.5, bf16[8,4096]{1,0:T(8,128)(2,1)S(1)} %copy-done), kind=kLoop, calls=%fused_computation | loop fusion | flops 98304 | bytes 262144 | tf_op jit(solution)/shard_map/convert_element_type | solution.py:400
  51.1 1.9 %copy.11 = bf16[512,512]{1,0:T(8,128)(2,1)} copy(bf16[512,512]{1,0:T(8,128)(2,1)} %get-tuple-element.9) | data formatting | bytes 1048576
Async XLA Ops:
  0.6 48.9 %copy-start = (bf16[8,4096]{1,0:T(8,128)(2,1)S(1)}, bf16[8,4096]{1,0:T(8,128)(2,1)}, u32[]{:S(2)}) copy-start(bf16[8,4096]{1,0:T(8,128)(2,1)} %tokens.1) | copy-start | bytes 196612
